TPU v7x, 128 devices: a whole 4x4x4 slice. The times are simulated.
128 devices in a mesh: rows: 32 (over z, y, core), cols: 4 (over x).
Axes of the slice: x: 4, y: 4, z: 4, core: 2. Of those that a mesh axis runs over, the one named last changes fastest.
Arguments:
- basis: float32 [64, 262144], P('cols', 'rows'), may hold values from -450 to 450
- blocks: bfloat16 [1024, 4, 256, 256], P('rows'), may hold values from -16 to 1, as said below
- far_cols: int32 [1024], P('rows'), may hold values from 0 to 1023, as said below
Outputs:
- basis_out: float32 [64, 262144], P('cols', 'rows')
- ritz: float32 [64, 64], P(None, 'cols')
Inputs may be any that keep to these rules, and one draw needn't show every extreme that they name: Off-diagonal entries are positive; each diagonal entry of a diagonal block is minus the sum of the other entries of its row over the four blocks, rounded to bfloat16. `far_cols`: the block rows of one device name at most 2 far columns among the block rows of any one device; the block rows of some device are named by exactly 2 block rows of every device.
All inputs are finite; a program needn't handle non-finite values.
Results may differ from a plain program's by a relative error of at most 0.0036.
Values may be sent and summed in bfloat16 or wider, within the bound.
No kernel may reach another device: no remote copies, remote signals or barrier semaphores. Data moves between devices by JAX's collectives and lax.ppermute only.
A program may use at most 128 MiB of HBM per device.

v0:
```python
import jax
import jax.numpy as jnp
from jax import lax
from jax.sharding import PartitionSpec as P

ITERS = 4


def with_halo(block, sides, width):
    for axis, dim in sides:
        count = lax.axis_size(axis)
        forward = [(i, i + 1) for i in range(count - 1)]
        forward.append((count - 1, 0))
        backward = [(target, source) for source, target in forward]
        low = lax.ppermute(
            lax.slice_in_dim(block, block.shape[dim] - width, None, axis=dim), axis, forward
        )
        high = lax.ppermute(lax.slice_in_dim(block, 0, width, axis=dim), axis, backward)
        block = jnp.concatenate([low, block, high], axis=dim)
    return block


def block_product(pieces, blocks, position):
    return jnp.einsum(
        "jbt,bst->jbs", pieces, blocks[:, position], preferred_element_type=jnp.float32
    )


def body(basis, blocks, far_cols):
    width = basis.shape[0]
    block_rows = blocks.shape[0]
    block_size = blocks.shape[2]
    row_devices = lax.axis_size("rows")
    total_states = block_rows * block_size * row_devices
    modes = width * lax.axis_size("cols")
    highest = lax.Precision.HIGHEST

    def apply_generator(iterate_bf):
        shaped = iterate_bf.reshape(width, block_rows, block_size)
        result = block_product(shaped, blocks, 0)
        empty = jnp.zeros((width, block_rows, block_size), jnp.bfloat16)
        piece = lax.all_gather(shaped, "rows", axis=1, tiled=True)
        inside = jnp.logical_and(far_cols >= 0, far_cols < piece.shape[1])
        taken = jnp.take(piece, jnp.clip(far_cols, 0, piece.shape[1] - 1), axis=1)
        remote = jnp.where(inside[None, :, None], taken, empty)
        extended = with_halo(shaped, (("rows", 1),), 1)
        result = result + block_product(extended[:, :-2], blocks, 1)
        result = result + block_product(extended[:, 2:], blocks, 2)
        result = result + block_product(remote, blocks, 3)
        return result.reshape(width, block_rows * block_size)

    iterate = basis
    for step in range(ITERS):
        iterate = iterate + 0.2 * apply_generator(iterate.astype(jnp.bfloat16))
    whole_iterate = lax.all_gather(iterate, "cols", axis=0, tiled=True)
    contract = (((1,), (1,)), ((), ()))
    gram_part = lax.dot_general(whole_iterate, iterate, contract, precision=highest)
    column_start = lax.axis_index("cols") * width
    gram_mine = lax.psum(gram_part, "rows")
    gram = lax.all_gather(gram_mine, "cols", axis=1, tiled=True) / total_states
    applied = apply_generator(iterate.astype(jnp.bfloat16))
    product_part = lax.dot_general(whole_iterate, applied, contract, precision=highest)
    product_mine = lax.psum(product_part, "rows")
    product = lax.all_gather(product_mine, "cols", axis=1, tiled=True) / total_states
    factor = jnp.linalg.cholesky(gram)
    identity_square = jnp.eye(modes, dtype=factor.dtype)
    inverse_factor = lax.linalg.triangular_solve(
        factor, identity_square, left_side=True, lower=True
    )
    own_rows = lax.dynamic_slice_in_dim(inverse_factor, column_start, width, 0)
    basis_out = jnp.dot(own_rows, whole_iterate, precision=highest)
    left_part = jnp.dot(inverse_factor, product, precision=highest)
    ritz_whole = jnp.dot(left_part, inverse_factor.T, precision=highest)
    ritz = lax.dynamic_slice_in_dim(ritz_whole, column_start, width, 1)
    return (basis_out, ritz)


def solution(mesh):
    in_specs = (P("cols", "rows"), P("rows", None, None, None), P("rows"))
    out_specs = (P("cols", "rows"), P(None, "cols"))
    return jax.shard_map(body, mesh=mesh, in_specs=in_specs, out_specs=out_specs, check_vma=False)
```

profile of v0, /device:TPU:0, one launch (start us, length us, event | category | flops | bytes accessed | tf_op | source)
XLA Modules:
  0.0 539.1 jit_solution(13265493274930220181)
XLA Ops:
  9.8 6.0 %collective-permute-start.1 = (bf16[16,1,256]{2,0,1:T(8,128)(2,1)S(1)}, bf16[16,1,256]{2,0,1:T(8,128)(2,1)S(1)}, u32[]{:S(2)}, u32[]{:S(2)}) collective-permute-start(bf16[16,1,256]{2,0,1:T(8,128)(2,1)S(1)} %get-tuple-element.23), channel_id=1, source_target_pairs={{4,0},{8,4},{12,8},{16,12},{20,16},{24,20},{28,24},{32,28},{36,32}... | collective-permute-start | bytes 24584 | tf_op jit(solution)/shard_map/ppermute | solution.py:18
  19.9 3.6 fusion.84
  23.5 3.5 fusion.81
  27.0 39.3 %all-gather.7.cloned.1.call-done = bf16[16,1024,256]{2,0,1:T(8,128)(2,1)} async-done(((bf16[16,32,256]{2,0,1:T(8,128)(2,1)}), bf16[16,1024,256]{2,0,1:T(8,128)(2,1)}) %all-gather.7.cloned.1.call-update) | async-done | bytes 8388624 | tf_op jit(solution)/shard_map/all_gather | solution.py:42
  66.4 3.9 gather_fusion
  81.6 3.6 fusion.16
  85.2 42.1 %all-gather.9.cloned.1.call-done = bf16[16,1024,256]{2,0,1:T(8,128)(2,1)} async-done(((bf16[16,32,256]{2,0,1:T(8,128)(2,1)}), bf16[16,1024,256]{2,0,1:T(8,128)(2,1)}) %all-gather.9.cloned.1.call-update) | async-done | bytes 8388624 | tf_op jit(solution)/shard_map/all_gather | solution.py:42
  127.3 3.9 gather_fusion.1
  145.9 3.6 fusion.14
  149.6 42.1 %all-gather.11.cloned.1.call-done = bf16[16,1024,256]{2,0,1:T(8,128)(2,1)} async-done(((bf16[16,32,256]{2,0,1:T(8,128)(2,1)}), bf16[16,1024,256]{2,0,1:T(8,128)(2,1)}) %all-gather.11.cloned.1.call-update) | async-done | bytes 8388624 | tf_op jit(solution)/shard_map/all_gather | solution.py:42
  191.6 3.9 gather_fusion.2
  210.3 3.6 fusion.12
  213.9 42.1 %all-gather.13.cloned.1.call-done = bf16[16,1024,256]{2,0,1:T(8,128)(2,1)} async-done(((bf16[16,32,256]{2,0,1:T(8,128)(2,1)}), bf16[16,1024,256]{2,0,1:T(8,128)(2,1)}) %all-gather.13.cloned.1.call-update) | async-done | bytes 8388624 | tf_op jit(solution)/shard_map/all_gather | solution.py:42
  256.0 3.9 gather_fusion.3
  275.5 3.8 fusion.10
  279.3 18.8 %all-gather.15.cloned.1.call-done = f32[64,8192]{1,0:T(8,128)} async-done(((f32[16,8192]{1,0:T(8,128)}), f32[64,8192]{1,0:T(8,128)}) %all-gather.15.cloned.1.call-update) | async-done | bytes 2097168 | tf_op jit(solution)/shard_map/all_gather | solution.py:55
  301.5 51.9 %all-gather.17.cloned.1.call-done = bf16[16,1024,256]{2,0,1:T(8,128)(2,1)} async-done(((bf16[16,32,256]{2,0,1:T(8,128)(2,1)}), bf16[16,1024,256]{2,0,1:T(8,128)(2,1)}) %all-gather.17.cloned.1.call-update) | async-done | bytes 8388624 | tf_op jit(solution)/shard_map/all_gather | solution.py:42
  353.3 3.9 gather_fusion.4
  360.7 3.6 fusion.105
  366.1 126.6 %all-reduce = (f32[64,16]{0,1:T(8,128)S(1)}, f32[64,16]{0,1:T(8,128)S(1)}) all-reduce(f32[64,16]{0,1:T(8,128)S(1)} %fusion.239, f32[64,16]{0,1:T(8,128)S(1)} %fusion.240), channel_id=1, replica_groups=mesh['rows'=32,'cols'=4] {'rows'}, use_global_device_ids=true, to_apply=%region_0.2 | all-reduce | flops 2048 | bytes 16384 | tf_op jit(solution)/shard_map/psum | solution.py:59
  492.6 12.4 %all_gather.29 = f32[64,64]{0,1:T(8,128)S(1)} all-gather(f32[64,16]{0,1:T(8,128)S(1)} %get-tuple-element.3), channel_id=1, replica_groups=mesh['rows'=32,'cols'=4] {'cols'}, dimensions={1}, use_global_device_ids=true | all-gather | bytes 20480 | tf_op jit(solution)/shard_map/all_gather | solution.py:60
  505.2 5.8 %cholesky.17 = f32[64,64]{1,0:T(8,128)S(1)} custom-call(f32[64,64]{1,0:T(8,128)S(1)} %fusion.202), custom_call_target="Cholesky" | custom-call | tf_op jit(solution)/shard_map/jit(cholesky)/cholesky | solution.py:65
  512.4 4.9 custom-call.6
  517.5 11.9 %all_gather.31 = f32[64,64]{0,1:T(8,128)S(1)} all-gather(f32[64,16]{0,1:T(8,128)S(1)} %get-tuple-element.4), channel_id=1, replica_groups=mesh['rows'=32,'cols'=4] {'cols'}, dimensions={1}, use_global_device_ids=true | all-gather | bytes 20480 | tf_op jit(solution)/shard_map/all_gather | solution.py:64
  (95 shorter events, 75.7 us)
Async XLA Ops:
  7.2 59.2 %all-gather.7.cloned.1.call-start = ((), (), s32[]{:S(2)}) async-start(), calls=%async_computation | async-start | bytes 8650752 | tf_op jit(solution)/shard_map/all_gather | solution.py:42
  9.0 118.3 %all-gather.9.cloned.1.call-start = ((), (), s32[]{:S(2)}) async-start(), calls=%async_computation.1 | async-start | bytes 8650752 | tf_op jit(solution)/shard_map/all_gather | solution.py:42
  9.8 10.1 %collective-permute-start = (bf16[16,1,256]{2,0,1:T(8,128)(2,1)S(1)}, bf16[16,1,256]{2,0,1:T(8,128)(2,1)S(1)}, u32[]{:S(2)}, u32[]{:S(2)}) collective-permute-start(bf16[16,1,256]{2,0,1:T(8,128)(2,1)S(1)} %get-tuple-element.24), channel_id=1, source_target_pairs={{0,4},{4,8},{8,12},{12,16},{16,20},{20,24},{24,28},{28,32},{32,36}... | collective-permute-start | bytes 24584 | tf_op jit(solution)/shard_map/ppermute | solution.py:15
  9.8 13.7 %collective-permute-start.1 = (bf16[16,1,256]{2,0,1:T(8,128)(2,1)S(1)}, bf16[16,1,256]{2,0,1:T(8,128)(2,1)S(1)}, u32[]{:S(2)}, u32[]{:S(2)}) collective-permute-start(bf16[16,1,256]{2,0,1:T(8,128)(2,1)S(1)} %get-tuple-element.23), channel_id=1, source_target_pairs={{4,0},{8,4},{12,8},{16,12},{20,16},{24,20},{28,24},{32,28},{36,32}... | collective-permute-start | bytes 24584 | tf_op jit(solution)/shard_map/ppermute | solution.py:18
  19.9 3.6 copy-start.4
  23.5 50.3 %copy-start.2 = (f32[16,8192]{1,0:T(8,128)S(1)}, f32[16,8192]{1,0:T(8,128)}, u32[]{:S(2)}) copy-start(f32[16,8192]{1,0:T(8,128)} %param.5) | copy-start | bytes 1572868
  74.6 117.0 %all-gather.11.cloned.1.call-start = ((), (), s32[]{:S(2)}) async-start(), calls=%async_computation.2 | async-start | bytes 8650752 | tf_op jit(solution)/shard_map/all_gather | solution.py:42
  75.4 6.2 %collective-permute-start.3 = (bf16[16,1,256]{2,0,1:T(8,128)(2,1)S(1)}, bf16[16,1,256]{2,0,1:T(8,128)(2,1)S(1)}, u32[]{:S(2)}, u32[]{:S(2)}) collective-permute-start(bf16[16,1,256]{2,0,1:T(8,128)(2,1)S(1)} %get-tuple-element.22), channel_id=1, source_target_pairs={{4,0},{8,4},{12,8},{16,12},{20,16},{24,20},{28,24},{32,28},{36,32}... | collective-permute-start | bytes 24584 | tf_op jit(solution)/shard_map/ppermute | solution.py:18
  81.6 53.1 %copy-start.5 = (bf16[2,32,8,256]{3,2,0,1:T(8,128)(2,1)S(1)}, bf16[2,32,8,256]{3,2,0,1:T(8,128)(2,1)}, u32[]{:S(2)}) copy-start(bf16[2,32,8,256]{3,2,0,1:T(8,128)(2,1)} %copy.157) | copy-start | bytes 786436
  81.6 53.1 %collective-permute-start.2 = (bf16[16,1,256]{2,0,1:T(8,128)(2,1)S(1)}, bf16[16,1,256]{2,0,1:T(8,128)(2,1)S(1)}, u32[]{:S(2)}, u32[]{:S(2)}) collective-permute-start(bf16[16,1,256]{2,0,1:T(8,128)(2,1)S(1)} %get-tuple-element.21), channel_id=1, source_target_pairs={{0,4},{4,8},{8,12},{12,16},{16,20},{20,24},{24,28},{28,32},{32,36}... | collective-permute-start | bytes 24584 | tf_op jit(solution)/shard_map/ppermute | solution.py:15
  138.9 117.0 %all-gather.13.cloned.1.call-start = ((), (), s32[]{:S(2)}) async-start(), calls=%async_computation.3 | async-start | bytes 8650752 | tf_op jit(solution)/shard_map/all_gather | solution.py:42
  139.7 6.2 %collective-permute-start.5 = (bf16[16,1,256]{2,0,1:T(8,128)(2,1)S(1)}, bf16[16,1,256]{2,0,1:T(8,128)(2,1)S(1)}, u32[]{:S(2)}, u32[]{:S(2)}) collective-permute-start(bf16[16,1,256]{2,0,1:T(8,128)(2,1)S(1)} %get-tuple-element.20), channel_id=1, source_target_pairs={{4,0},{8,4},{12,8},{16,12},{20,16},{24,20},{28,24},{32,28},{36,32}... | collective-permute-start | bytes 24584 | tf_op jit(solution)/shard_map/ppermute | solution.py:18
  145.9 53.1 %copy-start.6 = (bf16[2,32,8,256]{3,2,0,1:T(8,128)(2,1)S(1)}, bf16[2,32,8,256]{3,2,0,1:T(8,128)(2,1)}, u32[]{:S(2)}) copy-start(bf16[2,32,8,256]{3,2,0,1:T(8,128)(2,1)} %copy.156) | copy-start | bytes 786436
  145.9 53.1 %collective-permute-start.4 = (bf16[16,1,256]{2,0,1:T(8,128)(2,1)S(1)}, bf16[16,1,256]{2,0,1:T(8,128)(2,1)S(1)}, u32[]{:S(2)}, u32[]{:S(2)}) collective-permute-start(bf16[16,1,256]{2,0,1:T(8,128)(2,1)S(1)} %get-tuple-element.19), channel_id=1, source_target_pairs={{0,4},{4,8},{8,12},{12,16},{16,20},{20,24},{24,28},{28,32},{32,36}... | collective-permute-start | bytes 24584 | tf_op jit(solution)/shard_map/ppermute | solution.py:15
  203.3 94.9 %all-gather.15.cloned.1.call-start = ((), (), s32[]{:S(2)}) async-start(), calls=%async_computation.4 | async-start | bytes 2621440 | tf_op jit(solution)/shard_map/all_gather | solution.py:55
  204.0 6.2 %collective-permute-start.7 = (bf16[16,1,256]{2,0,1:T(8,128)(2,1)S(1)}, bf16[16,1,256]{2,0,1:T(8,128)(2,1)S(1)}, u32[]{:S(2)}, u32[]{:S(2)}) collective-permute-start(bf16[16,1,256]{2,0,1:T(8,128)(2,1)S(1)} %get-tuple-element.18), channel_id=1, source_target_pairs={{4,0},{8,4},{12,8},{16,12},{20,16},{24,20},{28,24},{32,28},{36,32}... | collective-permute-start | bytes 24584 | tf_op jit(solution)/shard_map/ppermute | solution.py:18
  210.3 53.1 %copy-start.7 = (bf16[2,32,8,256]{3,2,0,1:T(8,128)(2,1)S(1)}, bf16[2,32,8,256]{3,2,0,1:T(8,128)(2,1)}, u32[]{:S(2)}) copy-start(bf16[2,32,8,256]{3,2,0,1:T(8,128)(2,1)} %copy.155) | copy-start | bytes 786436
  210.3 53.1 %collective-permute-start.6 = (bf16[16,1,256]{2,0,1:T(8,128)(2,1)S(1)}, bf16[16,1,256]{2,0,1:T(8,128)(2,1)S(1)}, u32[]{:S(2)}, u32[]{:S(2)}) collective-permute-start(bf16[16,1,256]{2,0,1:T(8,128)(2,1)S(1)} %get-tuple-element.17), channel_id=1, source_target_pairs={{0,4},{4,8},{8,12},{12,16},{16,20},{20,24},{24,28},{28,32},{32,36}... | collective-permute-start | bytes 24584 | tf_op jit(solution)/shard_map/ppermute | solution.py:15
  267.7 85.7 %all-gather.17.cloned.1.call-start = ((), (), s32[]{:S(2)}) async-start(), calls=%async_computation.5 | async-start | bytes 8650752 | tf_op jit(solution)/shard_map/all_gather | solution.py:42
  269.2 6.2 %collective-permute-start.9 = (bf16[16,1,256]{2,0,1:T(8,128)(2,1)S(1)}, bf16[16,1,256]{2,0,1:T(8,128)(2,1)S(1)}, u32[]{:S(2)}, u32[]{:S(2)}) collective-permute-start(bf16[16,1,256]{2,0,1:T(8,128)(2,1)S(1)} %get-tuple-element.16), channel_id=1, source_target_pairs={{4,0},{8,4},{12,8},{16,12},{20,16},{24,20},{28,24},{32,28},{36,32}... | collective-permute-start | bytes 24584 | tf_op jit(solution)/shard_map/ppermute | solution.py:18
  275.4 22.7 %copy-start.1 = (f32[16,8192]{1,0:T(8,128)S(1)}, f32[16,8192]{1,0:T(8,128)}, u32[]{:S(2)}) copy-start(f32[16,8192]{1,0:T(8,128)} %get-tuple-element.6) | copy-start | bytes 1572868
  275.4 85.3 %copy-start.3 = (bf16[2,32,8,256]{3,2,0,1:T(8,128)(2,1)S(1)}, bf16[2,32,8,256]{3,2,0,1:T(8,128)(2,1)}, u32[]{:S(2)}) copy-start(bf16[2,32,8,256]{3,2,0,1:T(8,128)(2,1)} %copy.154) | copy-start | bytes 786436
  275.4 85.3 %collective-permute-start.8 = (bf16[16,1,256]{2,0,1:T(8,128)(2,1)S(1)}, bf16[16,1,256]{2,0,1:T(8,128)(2,1)S(1)}, u32[]{:S(2)}, u32[]{:S(2)}) collective-permute-start(bf16[16,1,256]{2,0,1:T(8,128)(2,1)S(1)} %get-tuple-element.15), channel_id=1, source_target_pairs={{0,4},{4,8},{8,12},{12,16},{16,20},{20,24},{24,28},{28,32},{32,36}... | collective-permute-start | bytes 24584 | tf_op jit(solution)/shard_map/ppermute | solution.py:15
  360.7 3.6 copy-start
Sparse Core Ops, SparseCore 0:
  10.8 55.4 all-gather.6
  74.7 52.5 all-gather.8
  139.1 52.5 all-gather.10
  203.4 52.5 all-gather.12
  267.8 30.2 all-gather.14
  300.2 53.0 all-gather.16
where the time goes:
time: 540 us; the launch traced here: 539 us
  waiting for transfers between devices  236 us (44%)
  blocking collectives  151 us (28%)
  matrix products  77.1 us (14%)
  local copies, waits for them, and re-layouts  27.9 us (5%)
  starting transfers between devices  17.6 us (3%)
  other arithmetic  14.9 us (3%)
  between operations  14.4 us (3%)
    all_gather x5, waiting for transfers between devices, apply_generator(): piece = lax.all_gather(shaped, 'rows', axis=1, tiled=True)  217 us
    psum x1, blocking collectives, body(): gram_mine = lax.psum(gram_part, 'rows')  127 us
    dot_general x20, matrix products, block_product(): jnp.einsum('jbt,bst->jbs', pieces, blocks[:, position], preferred_element...  69.5 us
    gather x5, local copies, waits for them, and re-layouts, apply_generator(): taken = jnp.take(piece, jnp.clip(far_cols, 0, piece.shape[1] - 1), axis=1)  19.7 us
    all_gather x1, waiting for transfers between devices, body(): whole_iterate = lax.all_gather(iterate, 'cols', axis=0, tiled=True)  18.8 us
    ppermute x5, starting transfers between devices, with_halo(): lax.ppermute(lax.slice_in_dim(block, 0, width, axis=dim), axis, backward)  17.3 us
    all_gather x1, blocking collectives, body(): gram = lax.all_gather(gram_mine, 'cols', axis=1, tiled=True) / total_states  12.4 us
    all_gather x1, blocking collectives, body(): lax.all_gather(product_mine, 'cols', axis=1, tiled=True) / total_states  11.9 us
  transfers between devices with their start and end apart: 16, of which 6 were waited for; matrix products, arithmetic and copies ran while one was open for 14% of the time, Pallas kernels for 0%

commit v1 on v0

--- a/solution.py
+++ b/solution.py
@@ -4,6 +4,11 @@
 from jax.sharding import PartitionSpec as P
 
 ITERS = 4
+
+
+def all_by_exchange(x, axis, dim):
+    sent = jnp.stack([x] * lax.axis_size(axis))
+    return jnp.concatenate(lax.all_to_all(sent, axis, 0, 0), axis=dim)
 
 
 def with_halo(block, sides, width):
@@ -57,7 +62,7 @@
     gram_part = lax.dot_general(whole_iterate, iterate, contract, precision=highest)
     column_start = lax.axis_index("cols") * width
     gram_mine = lax.psum(gram_part, "rows")
-    gram = lax.all_gather(gram_mine, "cols", axis=1, tiled=True) / total_states
+    gram = all_by_exchange(gram_mine, "cols", 1) / total_states
     applied = apply_generator(iterate.astype(jnp.bfloat16))
     product_part = lax.dot_general(whole_iterate, applied, contract, precision=highest)
     product_mine = lax.psum(product_part, "rows")

time: 540 us -> 535 us (level)
  blocking collectives: 151 us -> 140 us
    all_gather x1 -> x0, blocking collectives: 12.4 us -> none  [body(): gram = lax.all_gather(gram_mine, 'cols', axis=1, tiled=True) / total_states]
  transfers between devices with their start and end apart: 16 -> 17, of which waited for: 6 -> 6; matrix products, arithmetic and copies ran while one was open for 14% -> 14% of each run, Pallas kernels for 0% -> 0%
where the time goes in v1:
time: 535 us; the launch traced here: 534 us
  waiting for transfers between devices  236 us (44%)
  blocking collectives  140 us (26%)
  matrix products  77.1 us (14%)
  local copies, waits for them, and re-layouts  29.2 us (5%)
  starting transfers between devices  21.8 us (4%)
  other arithmetic  15.6 us (3%)
  between operations  14.4 us (3%)
    all_gather x5, waiting for transfers between devices, apply_generator(): piece = lax.all_gather(shaped, 'rows', axis=1, tiled=True)  217 us
    psum x1, blocking collectives, body(): gram_mine = lax.psum(gram_part, 'rows')  127 us
    dot_general x20, matrix products, block_product(): jnp.einsum('jbt,bst->jbs', pieces, blocks[:, position], preferred_element...  69.5 us
    gather x5, local copies, waits for them, and re-layouts, apply_generator(): taken = jnp.take(piece, jnp.clip(far_cols, 0, piece.shape[1] - 1), axis=1)  19.7 us
    all_gather x1, waiting for transfers between devices, body(): whole_iterate = lax.all_gather(iterate, 'cols', axis=0, tiled=True)  18.8 us
    ppermute x5, starting transfers between devices, with_halo(): lax.ppermute(lax.slice_in_dim(block, 0, width, axis=dim), axis, backward)  17.3 us
    all_gather x1, blocking collectives, body(): lax.all_gather(product_mine, 'cols', axis=1, tiled=True) / total_states  13 us
  transfers between devices with their start and end apart: 17, of which 6 were waited for; matrix products, arithmetic and copies ran while one was open for 14% of the time, Pallas kernels for 0%

profile of v1, /device:TPU:0, one launch (start us, length us, event | category | flops | bytes accessed | tf_op | source)
XLA Modules:
  0.0 534.0 jit_solution(4215045404753814674)
XLA Ops:
  9.8 6.0 %collective-permute-start.1 = (bf16[16,1,256]{2,0,1:T(8,128)(2,1)S(1)}, bf16[16,1,256]{2,0,1:T(8,128)(2,1)S(1)}, u32[]{:S(2)}, u32[]{:S(2)}) collective-permute-start(bf16[16,1,256]{2,0,1:T(8,128)(2,1)S(1)} %get-tuple-element.23), channel_id=1, source_target_pairs={{4,0},{8,4},{12,8},{16,12},{20,16},{24,20},{28,24},{32,28},{36,32}... | collective-permute-start | bytes 24584 | tf_op jit(solution)/shard_map/ppermute | solution.py:23
  19.9 3.6 fusion.84
  23.5 3.5 fusion.81
  27.0 39.3 %all-gather.7.cloned.1.call-done = bf16[16,1024,256]{2,0,1:T(8,128)(2,1)} async-done(((bf16[16,32,256]{2,0,1:T(8,128)(2,1)}), bf16[16,1024,256]{2,0,1:T(8,128)(2,1)}) %all-gather.7.cloned.1.call-update) | async-done | bytes 8388624 | tf_op jit(solution)/shard_map/all_gather | solution.py:47
  66.4 3.9 gather_fusion
  81.6 3.6 fusion.16
  85.2 42.1 %all-gather.9.cloned.1.call-done = bf16[16,1024,256]{2,0,1:T(8,128)(2,1)} async-done(((bf16[16,32,256]{2,0,1:T(8,128)(2,1)}), bf16[16,1024,256]{2,0,1:T(8,128)(2,1)}) %all-gather.9.cloned.1.call-update) | async-done | bytes 8388624 | tf_op jit(solution)/shard_map/all_gather | solution.py:47
  127.3 3.9 gather_fusion.1
  146.0 3.6 fusion.14
  149.6 42.1 %all-gather.11.cloned.1.call-done = bf16[16,1024,256]{2,0,1:T(8,128)(2,1)} async-done(((bf16[16,32,256]{2,0,1:T(8,128)(2,1)}), bf16[16,1024,256]{2,0,1:T(8,128)(2,1)}) %all-gather.11.cloned.1.call-update) | async-done | bytes 8388624 | tf_op jit(solution)/shard_map/all_gather | solution.py:47
  191.6 3.9 gather_fusion.2
  210.3 3.6 fusion.12
  213.9 42.1 %all-gather.13.cloned.1.call-done = bf16[16,1024,256]{2,0,1:T(8,128)(2,1)} async-done(((bf16[16,32,256]{2,0,1:T(8,128)(2,1)}), bf16[16,1024,256]{2,0,1:T(8,128)(2,1)}) %all-gather.13.cloned.1.call-update) | async-done | bytes 8388624 | tf_op jit(solution)/shard_map/all_gather | solution.py:47
  256.0 3.9 gather_fusion.3
  275.5 3.8 fusion.10
  279.3 18.8 %all-gather.15.cloned.1.call-done = f32[64,8192]{1,0:T(8,128)} async-done(((f32[16,8192]{1,0:T(8,128)}), f32[64,8192]{1,0:T(8,128)}) %all-gather.15.cloned.1.call-update) | async-done | bytes 2097168 | tf_op jit(solution)/shard_map/all_gather | solution.py:60
  301.5 51.9 %all-gather.17.cloned.1.call-done = bf16[16,1024,256]{2,0,1:T(8,128)(2,1)} async-done(((bf16[16,32,256]{2,0,1:T(8,128)(2,1)}), bf16[16,1024,256]{2,0,1:T(8,128)(2,1)}) %all-gather.17.cloned.1.call-update) | async-done | bytes 8388624 | tf_op jit(solution)/shard_map/all_gather | solution.py:47
  353.4 3.9 gather_fusion.4
  360.8 3.5 fusion.105
  366.1 126.6 %all-reduce = (f32[64,16]{0,1:T(8,128)S(1)}, f32[64,16]{0,1:T(8,128)S(1)}) all-reduce(f32[64,16]{0,1:T(8,128)S(1)} %fusion.239, f32[64,16]{0,1:T(8,128)S(1)} %fusion.240), channel_id=1, replica_groups=mesh['rows'=32,'cols'=4] {'rows'}, use_global_device_ids=true, to_apply=%region_0.2 | all-reduce | flops 2048 | bytes 16384 | tf_op jit(solution)/shard_map/psum | solution.py:64
  493.4 4.2 all-to-all-start
  497.6 13.0 %all_gather.27 = f32[64,64]{0,1:T(8,128)S(1)} all-gather(f32[64,16]{0,1:T(8,128)S(1)} %get-tuple-element.4), channel_id=1, replica_groups=mesh['rows'=32,'cols'=4] {'cols'}, dimensions={1}, use_global_device_ids=true | all-gather | bytes 20480 | tf_op jit(solution)/shard_map/all_gather | solution.py:69
  512.0 5.8 %cholesky.17 = f32[64,64]{1,0:T(8,128)S(1)} custom-call(f32[64,64]{1,0:T(8,128)S(1)} %fusion.200), custom_call_target="Cholesky" | custom-call | tf_op jit(solution)/shard_map/jit(cholesky)/cholesky | solution.py:70
  519.2 4.9 custom-call.6
  (101 shorter events, 77.7 us)
Async XLA Ops:
  7.2 59.2 %all-gather.7.cloned.1.call-start = ((), (), s32[]{:S(2)}) async-start(), calls=%async_computation.1 | async-start | bytes 8650752 | tf_op jit(solution)/shard_map/all_gather | solution.py:47
  9.0 118.3 %all-gather.9.cloned.1.call-start = ((), (), s32[]{:S(2)}) async-start(), calls=%async_computation.2 | async-start | bytes 8650752 | tf_op jit(solution)/shard_map/all_gather | solution.py:47
  9.8 10.1 %collective-permute-start = (bf16[16,1,256]{2,0,1:T(8,128)(2,1)S(1)}, bf16[16,1,256]{2,0,1:T(8,128)(2,1)S(1)}, u32[]{:S(2)}, u32[]{:S(2)}) collective-permute-start(bf16[16,1,256]{2,0,1:T(8,128)(2,1)S(1)} %get-tuple-element.24), channel_id=1, source_target_pairs={{0,4},{4,8},{8,12},{12,16},{16,20},{20,24},{24,28},{28,32},{32,36}... | collective-permute-start | bytes 24584 | tf_op jit(solution)/shard_map/ppermute | solution.py:20
  9.8 13.7 %collective-permute-start.1 = (bf16[16,1,256]{2,0,1:T(8,128)(2,1)S(1)}, bf16[16,1,256]{2,0,1:T(8,128)(2,1)S(1)}, u32[]{:S(2)}, u32[]{:S(2)}) collective-permute-start(bf16[16,1,256]{2,0,1:T(8,128)(2,1)S(1)} %get-tuple-element.23), channel_id=1, source_target_pairs={{4,0},{8,4},{12,8},{16,12},{20,16},{24,20},{28,24},{32,28},{36,32}... | collective-permute-start | bytes 24584 | tf_op jit(solution)/shard_map/ppermute | solution.py:23
  23.5 50.3 %copy-start.2 = (f32[16,8192]{1,0:T(8,128)S(1)}, f32[16,8192]{1,0:T(8,128)}, u32[]{:S(2)}) copy-start(f32[16,8192]{1,0:T(8,128)} %param.5) | copy-start | bytes 1572868
  74.6 117.0 %all-gather.11.cloned.1.call-start = ((), (), s32[]{:S(2)}) async-start(), calls=%async_computation.3 | async-start | bytes 8650752 | tf_op jit(solution)/shard_map/all_gather | solution.py:47
  75.4 6.2 %collective-permute-start.3 = (bf16[16,1,256]{2,0,1:T(8,128)(2,1)S(1)}, bf16[16,1,256]{2,0,1:T(8,128)(2,1)S(1)}, u32[]{:S(2)}, u32[]{:S(2)}) collective-permute-start(bf16[16,1,256]{2,0,1:T(8,128)(2,1)S(1)} %get-tuple-element.22), channel_id=1, source_target_pairs={{4,0},{8,4},{12,8},{16,12},{20,16},{24,20},{28,24},{32,28},{36,32}... | collective-permute-start | bytes 24584 | tf_op jit(solution)/shard_map/ppermute | solution.py:23
  81.6 53.1 %copy-start.5 = (bf16[2,32,8,256]{3,2,0,1:T(8,128)(2,1)S(1)}, bf16[2,32,8,256]{3,2,0,1:T(8,128)(2,1)}, u32[]{:S(2)}) copy-start(bf16[2,32,8,256]{3,2,0,1:T(8,128)(2,1)} %copy.157) | copy-start | bytes 786436
  81.6 53.1 %collective-permute-start.2 = (bf16[16,1,256]{2,0,1:T(8,128)(2,1)S(1)}, bf16[16,1,256]{2,0,1:T(8,128)(2,1)S(1)}, u32[]{:S(2)}, u32[]{:S(2)}) collective-permute-start(bf16[16,1,256]{2,0,1:T(8,128)(2,1)S(1)} %get-tuple-element.21), channel_id=1, source_target_pairs={{0,4},{4,8},{8,12},{12,16},{16,20},{20,24},{24,28},{28,32},{32,36}... | collective-permute-start | bytes 24584 | tf_op jit(solution)/shard_map/ppermute | solution.py:20
  139.0 117.0 %all-gather.13.cloned.1.call-start = ((), (), s32[]{:S(2)}) async-start(), calls=%async_computation.4 | async-start | bytes 8650752 | tf_op jit(solution)/shard_map/all_gather | solution.py:47
  139.7 6.2 %collective-permute-start.5 = (bf16[16,1,256]{2,0,1:T(8,128)(2,1)S(1)}, bf16[16,1,256]{2,0,1:T(8,128)(2,1)S(1)}, u32[]{:S(2)}, u32[]{:S(2)}) collective-permute-start(bf16[16,1,256]{2,0,1:T(8,128)(2,1)S(1)} %get-tuple-element.20), channel_id=1, source_target_pairs={{4,0},{8,4},{12,8},{16,12},{20,16},{24,20},{28,24},{32,28},{36,32}... | collective-permute-start | bytes 24584 | tf_op jit(solution)/shard_map/ppermute | solution.py:23
  145.9 53.1 %copy-start.6 = (bf16[2,32,8,256]{3,2,0,1:T(8,128)(2,1)S(1)}, bf16[2,32,8,256]{3,2,0,1:T(8,128)(2,1)}, u32[]{:S(2)}) copy-start(bf16[2,32,8,256]{3,2,0,1:T(8,128)(2,1)} %copy.156) | copy-start | bytes 786436
  145.9 53.1 %collective-permute-start.4 = (bf16[16,1,256]{2,0,1:T(8,128)(2,1)S(1)}, bf16[16,1,256]{2,0,1:T(8,128)(2,1)S(1)}, u32[]{:S(2)}, u32[]{:S(2)}) collective-permute-start(bf16[16,1,256]{2,0,1:T(8,128)(2,1)S(1)} %get-tuple-element.19), channel_id=1, source_target_pairs={{0,4},{4,8},{8,12},{12,16},{16,20},{20,24},{24,28},{28,32},{32,36}... | collective-permute-start | bytes 24584 | tf_op jit(solution)/shard_map/ppermute | solution.py:20
  203.3 94.9 %all-gather.15.cloned.1.call-start = ((), (), s32[]{:S(2)}) async-start(), calls=%async_computation.5 | async-start | bytes 2621440 | tf_op jit(solution)/shard_map/all_gather | solution.py:60
  204.1 6.2 %collective-permute-start.7 = (bf16[16,1,256]{2,0,1:T(8,128)(2,1)S(1)}, bf16[16,1,256]{2,0,1:T(8,128)(2,1)S(1)}, u32[]{:S(2)}, u32[]{:S(2)}) collective-permute-start(bf16[16,1,256]{2,0,1:T(8,128)(2,1)S(1)} %get-tuple-element.18), channel_id=1, source_target_pairs={{4,0},{8,4},{12,8},{16,12},{20,16},{24,20},{28,24},{32,28},{36,32}... | collective-permute-start | bytes 24584 | tf_op jit(solution)/shard_map/ppermute | solution.py:23
  210.3 53.1 %copy-start.7 = (bf16[2,32,8,256]{3,2,0,1:T(8,128)(2,1)S(1)}, bf16[2,32,8,256]{3,2,0,1:T(8,128)(2,1)}, u32[]{:S(2)}) copy-start(bf16[2,32,8,256]{3,2,0,1:T(8,128)(2,1)} %copy.155) | copy-start | bytes 786436
  210.3 53.1 %collective-permute-start.6 = (bf16[16,1,256]{2,0,1:T(8,128)(2,1)S(1)}, bf16[16,1,256]{2,0,1:T(8,128)(2,1)S(1)}, u32[]{:S(2)}, u32[]{:S(2)}) collective-permute-start(bf16[16,1,256]{2,0,1:T(8,128)(2,1)S(1)} %get-tuple-element.17), channel_id=1, source_target_pairs={{0,4},{4,8},{8,12},{12,16},{16,20},{20,24},{24,28},{28,32},{32,36}... | collective-permute-start | bytes 24584 | tf_op jit(solution)/shard_map/ppermute | solution.py:20
  267.7 85.7 %all-gather.17.cloned.1.call-start = ((), (), s32[]{:S(2)}) async-start(), calls=%async_computation.6 | async-start | bytes 8650752 | tf_op jit(solution)/shard_map/all_gather | solution.py:47
  269.2 6.3 %collective-permute-start.9 = (bf16[16,1,256]{2,0,1:T(8,128)(2,1)S(1)}, bf16[16,1,256]{2,0,1:T(8,128)(2,1)S(1)}, u32[]{:S(2)}, u32[]{:S(2)}) collective-permute-start(bf16[16,1,256]{2,0,1:T(8,128)(2,1)S(1)} %get-tuple-element.16), channel_id=1, source_target_pairs={{4,0},{8,4},{12,8},{16,12},{20,16},{24,20},{28,24},{32,28},{36,32}... | collective-permute-start | bytes 24584 | tf_op jit(solution)/shard_map/ppermute | solution.py:23
  275.4 22.8 %copy-start.1 = (f32[16,8192]{1,0:T(8,128)S(1)}, f32[16,8192]{1,0:T(8,128)}, u32[]{:S(2)}) copy-start(f32[16,8192]{1,0:T(8,128)} %get-tuple-element.6) | copy-start | bytes 1572868
  275.4 85.3 %copy-start.3 = (bf16[2,32,8,256]{3,2,0,1:T(8,128)(2,1)S(1)}, bf16[2,32,8,256]{3,2,0,1:T(8,128)(2,1)}, u32[]{:S(2)}) copy-start(bf16[2,32,8,256]{3,2,0,1:T(8,128)(2,1)} %copy.154) | copy-start | bytes 786436
  275.4 85.3 %collective-permute-start.8 = (bf16[16,1,256]{2,0,1:T(8,128)(2,1)S(1)}, bf16[16,1,256]{2,0,1:T(8,128)(2,1)S(1)}, u32[]{:S(2)}, u32[]{:S(2)}) collective-permute-start(bf16[16,1,256]{2,0,1:T(8,128)(2,1)S(1)} %get-tuple-element.15), channel_id=1, source_target_pairs={{0,4},{4,8},{8,12},{12,16},{16,20},{20,24},{24,28},{28,32},{32,36}... | collective-permute-start | bytes 24584 | tf_op jit(solution)/shard_map/ppermute | solution.py:20
  360.7 3.6 copy-start
  493.4 17.2 %all-to-all-start = ((f32[4,1,1024]{2,1,0:T(1,128)}), f32[4,1,1024]{2,1,0:T(1,128)S(1)}, u32[]{:S(2)}, u32[]{:S(2)}) async-start(f32[4,1,1024]{2,1,0:T(1,128)} %reshape.116), calls=%async_computation | async-start | bytes 32768 | tf_op jit(solution)/shard_map/all_to_all | solution.py:11
  (1 other events, 3.6 us)
Sparse Core Ops, SparseCore 0:
  10.8 55.4 all-gather.6
  74.7 52.5 all-gather.8
  139.1 52.5 all-gather.10
  203.4 52.5 all-gather.12
  267.8 30.2 all-gather.14
  300.3 53.0 all-gather.16
